TPU v7x, 128 devices: a whole 4x4x4 slice. The times are simulated.
128 devices in a mesh: seq: 16 (over z, y), expert: 8 (over x, core).
Axes of the slice: x: 4, y: 4, z: 4, core: 2. Of those that a mesh axis runs over, the one named last changes fastest.
Arguments:
- tokens: bfloat16 [2048, 4096], P(('seq', 'expert')), may hold values from -6 to 6
- gain_mamba: float32 [4096], replicated, may hold values from 0.1 to 1.9
- in_weight: bfloat16 [2, 4096, 8192], P(None, 'seq', 'expert'), may hold values from -0.09375 to 0.09375
- conv_weight: float32 [4, 8192], P(None, 'expert'), may hold values from -3 to 3
- conv_bias: float32 [8192], P('expert'), may hold values from -3 to 3
- xproj_weight: bfloat16 [8192, 288], P('expert'), may hold values from -0.0625 to 0.0625
- dt_weight: bfloat16 [256, 8192], P(None, 'expert'), may hold values from -0.375 to 0.375
- dt_bias: float32 [8192], P('expert'), may hold values from -7 to -2
- a_rate: float32 [16, 8192], P(None, 'expert'), may hold values from 0.01 to 8
- skip_d: float32 [8192], P('expert'), may hold values from 0.5 to 1.5
- out_weight: bfloat16 [8192, 4096], P('expert', 'seq'), may hold values from -0.0625 to 0.0625
- gain_moe: float32 [4096], replicated, may hold values from 0.1 to 1.9
- expert_ids: int32 [2048, 2], P(('seq', 'expert')), may hold values from 0 to 15, all different within a row; in each aligned block of 16 rows (0 to 15, 16 to 31, ...) at most 4 rows name the same one
- gate_weights: float32 [2048, 2], P(('seq', 'expert')), may hold values from 0.2 to 1
- w_gate: bfloat16 [16, 4096, 7168], P('seq', None, 'expert'), may hold values from -0.09375 to 0.09375
- w_up: bfloat16 [16, 4096, 7168], P('seq', None, 'expert'), may hold values from -0.09375 to 0.09375
- w_down: bfloat16 [16, 7168, 4096], P('seq', 'expert'), may hold values from -0.0625 to 0.0625
Outputs:
- mixed: bfloat16 [2048, 4096], P(('seq', 'expert'))
Inputs may be any that keep to these rules, and one draw needn't show every extreme that they name: `expert_ids`: each row names 2 different experts. In each aligned block of 16 rows (the rows of one device) no expert is named by more than 4 rows, a bound that some block reaches.
All inputs are finite; a program needn't handle non-finite values.
Results may differ from a plain program's by a relative error of at most 0.03.
Values may be sent and summed in bfloat16 or wider, within the bound.
A program may use at most 192 MiB of HBM per device.

v0:
```python
import jax
import jax.numpy as jnp
from jax import lax
from jax.sharding import PartitionSpec as P

STATE = 16
CONV = 4
RANK = 256
TOP = 2


def from_behind(block, axis, distance):
    devices = range(lax.axis_size(axis))
    route = [(i - distance, i) for i in devices if i - distance in devices]
    return lax.ppermute(block, axis, route)


def rms_norm(values, gain):
    wide = values.astype(jnp.float32)
    return wide * lax.rsqrt(jnp.mean(wide * wide, axis=-1, keepdims=True) + 1e-05) * gain


def combine_states(earlier, later):
    return (earlier[0] * later[0], later[0] * earlier[1] + later[1])


def per_device(
    tokens,
    gain_mamba,
    in_weight,
    conv_weight,
    conv_bias,
    xproj_weight,
    dt_weight,
    dt_bias,
    a_rate,
    skip_d,
    out_weight,
    gain_moe,
    expert_ids,
    gate_weights,
    w_gate,
    w_up,
    w_down,
):
    rows, dim = tokens.shape
    n_seq = lax.axis_size("seq")
    n_exp = lax.axis_size("expert")
    group = lax.all_gather(tokens, "expert", axis=0, tiled=True)
    local_tok = group.shape[0]
    normed = rms_norm(group, gain_mamba).astype(jnp.bfloat16)
    both = jnp.einsum(
        "td,kdc->tkc",
        normed,
        lax.all_gather(in_weight, "seq", axis=1, tiled=True),
        preferred_element_type=jnp.float32,
    )
    xpart = both[:, 0]
    zpart = both[:, 1]
    edge = from_behind(xpart[local_tok - (CONV - 1) :], "seq", 1)
    padded = jnp.concatenate([edge, xpart], axis=0)
    conv = conv_bias
    for tap in range(CONV):
        conv = conv + conv_weight[tap] * padded[tap : tap + local_tok]
    inner = jax.nn.silu(conv).astype(jnp.bfloat16)
    partial_value = jnp.dot(inner, xproj_weight, preferred_element_type=jnp.float32)
    low_part, edge_part = (
        lax.psum(partial_value[:, :RANK].astype(jnp.bfloat16), "expert").astype(jnp.float32),
        lax.psum(partial_value[:, RANK:].astype(jnp.bfloat16), "expert").astype(jnp.float32),
    )
    dt_low = low_part.astype(jnp.bfloat16)
    bmat = edge_part[:, :STATE]
    cmat = edge_part[:, STATE:]
    step = jax.nn.softplus(jnp.dot(dt_low, dt_weight, preferred_element_type=jnp.float32) + dt_bias)
    inner_f = inner.astype(jnp.float32)
    decay = jnp.exp(-step[:, None, :] * a_rate[None, :, :])
    source = bmat[:, :, None] * (step * inner_f)[:, None, :]
    cumulative, states = lax.associative_scan(combine_states, (decay, source), axis=0)
    total = cumulative[-1]
    final = states[-1]

    def relay(turn, incoming):
        return from_behind((total * incoming + final).astype(jnp.bfloat16), "seq", 1).astype(
            jnp.float32
        )

    arriving = lax.fori_loop(0, n_seq - 1, relay, jnp.zeros_like(final))
    states = states + cumulative * arriving[None, :, :]
    readout = jnp.sum(cmat[:, :, None] * states, axis=1)
    gated = ((readout + skip_d * inner_f) * jax.nn.silu(zpart)).astype(jnp.bfloat16)
    terms = jnp.dot(
        gated,
        lax.all_gather(out_weight, "seq", axis=1, tiled=True),
        preferred_element_type=jnp.float32,
    )
    mixer = lax.psum_scatter(
        terms.astype(jnp.bfloat16), "expert", scatter_dimension=0, tiled=True
    ).astype(jnp.float32)
    resid = (tokens.astype(jnp.float32) + mixer).astype(jnp.bfloat16)
    normed2 = rms_norm(resid, gain_moe).astype(jnp.bfloat16)
    capacity = max(2, 4 * rows // n_seq)
    slots_all = n_seq * capacity
    flat_ids = expert_ids.reshape(-1)
    onehot = (flat_ids[:, None] == jnp.arange(n_seq, dtype=jnp.int32)[None, :]).astype(jnp.int32)
    before = jnp.cumsum(onehot, axis=0) - onehot
    slot = jnp.sum(before * onehot, axis=1)
    target = flat_ids * capacity + slot
    places = target[:, None] == jnp.arange(slots_all, dtype=jnp.int32)[None, :]
    dispatch_mat = jnp.any(places.reshape(rows, TOP, slots_all), axis=1).astype(jnp.bfloat16)
    send = jnp.einsum(
        "rp,rd->pd", dispatch_mat, normed2, preferred_element_type=jnp.float32
    ).astype(jnp.bfloat16)
    received = lax.all_to_all(
        send.reshape(n_seq, capacity, dim), "seq", split_axis=0, concat_axis=0, tiled=True
    )
    pooled = lax.all_gather(
        received.reshape(1, slots_all, dim), "expert", axis=0, tiled=True
    ).reshape(n_exp * slots_all, dim)
    gate = jnp.dot(pooled, w_gate[0], preferred_element_type=jnp.float32)
    upper = jnp.dot(pooled, w_up[0], preferred_element_type=jnp.float32)
    act = (jax.nn.silu(gate) * upper).astype(jnp.bfloat16)
    outputs = lax.psum_scatter(
        jnp.dot(act, w_down[0], preferred_element_type=jnp.float32).astype(jnp.bfloat16),
        "expert",
        scatter_dimension=0,
        tiled=True,
    )
    returned = lax.all_to_all(
        outputs.reshape(n_seq, capacity, dim), "seq", split_axis=0, concat_axis=0, tiled=True
    ).reshape(slots_all, dim)
    weighting = jnp.where(places, gate_weights.reshape(-1)[:, None], 0.0)
    weighting = jnp.sum(weighting.reshape(rows, TOP, slots_all), axis=1)
    moe = jnp.dot(weighting, returned.astype(jnp.float32), precision=lax.Precision.HIGHEST)
    return (resid.astype(jnp.float32) + moe).astype(jnp.bfloat16)


def solution(mesh):
    placed = (
        P(("seq", "expert"), None),
        P(),
        P(None, "seq", "expert"),
        P(None, "expert"),
        P("expert"),
        P("expert", None),
        P(None, "expert"),
        P("expert"),
        P(None, "expert"),
        P("expert"),
        P("expert", "seq"),
        P(),
        P(("seq", "expert"), None),
        P(("seq", "expert"), None),
        P("seq", None, "expert"),
        P("seq", None, "expert"),
        P("seq", "expert", None),
    )
    return jax.shard_map(
        per_device,
        mesh=mesh,
        in_specs=placed,
        out_specs=P(("seq", "expert"), None),
        check_vma=False,
    )
```

profile of v0, /device:TPU:0, one launch (start us, length us, event | category | flops | bytes accessed | tf_op | source)
XLA Modules:
  0.0 908.5 jit_solution(7577490913799089768)
XLA Ops:
  8.9 26.0 %all-gather.5.cloned.1.call-done = bf16[128,4096]{1,0:T(8,128)(2,1)} async-done(((bf16[16,4096]{1,0:T(8,128)(2,1)}), bf16[128,4096]{1,0:T(8,128)(2,1)}) %all-gather.5.cloned.1.call-update) | async-done | bytes 1048592 | tf_op jit(solution)/shard_map/all_gather | solution.py:49
  36.5 111.9 %all-gather.7.cloned.1.call-done = bf16[2,4096,1024]{2,1,0:T(8,128)(2,1)} async-done(((bf16[2,256,1024]{2,1,0:T(8,128)(2,1)}), bf16[2,4096,1024]{2,1,0:T(8,128)(2,1)}) %all-gather.7.cloned.1.call-update) | async-done | bytes 16777232 | tf_op jit(solution)/shard_map/all_gather | solution.py:55
  148.4 8.5 fusion.20
  163.9 14.0 %psum.14 = bf16[128,32]{0,1:T(8,128)(2,1)S(1)} all-reduce(bf16[128,32]{0,1:T(8,128)(2,1)S(1)} %slice.341), channel_id=1, replica_groups=mesh['seq'=16,'expert'=8] {'expert'}, use_global_device_ids=true, to_apply=%region_1.2 | all-reduce | flops 4096 | bytes 16384 | tf_op jit(solution)/shard_map/psum | solution.py:69
  178.7 44.8 %all-reduce.30.cloned.1.call-done = bf16[128,256]{0,1:T(8,128)(2,1)} async-done(((bf16[128,256]{0,1:T(8,128)(2,1)}), bf16[128,256]{0,1:T(8,128)(2,1)}) %all-reduce.30.cloned.1.call-update) | async-done | bytes 65552 | tf_op jit(solution)/shard_map/psum | solution.py:68
  233.5 10.9 %slice_add_fusion = (f32[64,16,1024]{2,1,0:T(8,128)S(1)}, f32[64,16,1024]{2,1,0:T(8,128)}) fusion(f32[128,16,1024]{2,1,0:T(8,128)} %copy-done.3, f32[128,16,1024]{2,1,0:T(8,128)} %copy-done.2), kind=kLoop, calls=%fused_computation.19 | loop fusion | flops 3145728 | bytes 25165824 | tf_op jit(solution)/shard_map/add | solution.py:24
  308.4 7.0 pad.108
  315.3 10.2 %pad.109 = f32[32,16,1024]{2,1,0:T(8,128)} pad(f32[16,16,1024]{2,1,0:T(8,128)} %add.263, f32[]{:T(128)} %constant.13.clone.1), padding=1_0_1x0_0_0x0_0_0 | pad | bytes 3145732 | tf_op jit(solution)/shard_map/pad | solution.py:78
  325.5 10.1 %pad.95 = f32[32,16,1024]{2,1,0:T(8,128)} pad(f32[16,16,1024]{2,1,0:T(8,128)} %add.253, f32[]{:T(128)} %constant.13.clone.1), padding=1_0_1x0_0_0x0_0_0 | pad | bytes 3145732 | tf_op jit(solution)/shard_map/pad | solution.py:78
  337.9 10.2 %pad.94 = f32[32,16,1024]{2,1,0:T(8,128)} pad(f32[16,16,1024]{2,1,0:T(8,128)} %pad_maximum_fusion.4, f32[]{:T(128)} %constant.13.clone.1), padding=0_1_1x0_0_0x0_0_0 | pad | bytes 3145732 | tf_op jit(solution)/shard_map/pad | solution.py:78
  348.1 4.3 add.255
  355.3 5.0 fusion.16
  362.0 18.6 %pad.96 = f32[64,16,1024]{2,1,0:T(8,128)} pad(f32[32,16,1024]{2,1,0:T(8,128)} %pad_maximum_fusion.2, f32[]{:T(128)} %constant.13.clone.1), padding=0_1_1x0_0_0x0_0_0 | pad | bytes 6291460 | tf_op jit(solution)/shard_map/pad | solution.py:78
  380.6 12.0 %pad.97 = f32[64,16,1024]{2,1,0:T(8,128)} pad(f32[32,16,1024]{2,1,0:T(8,128)S(1)} %copy-done.16, f32[]{:T(128)} %constant.13.clone.1), padding=1_0_1x0_0_0x0_0_0 | pad | bytes 6291460 | tf_op jit(solution)/shard_map/pad | solution.py:78
  392.5 6.8 add.257
  399.4 35.6 %pad.99 = f32[128,16,1024]{2,1,0:T(8,128)} pad(f32[64,16,1024]{2,1,0:T(8,128)} %add.257, f32[]{:T(128)} %constant.13.clone.1), padding=1_0_1x0_0_0x0_0_0 | pad | bytes 12582916 | tf_op jit(solution)/shard_map/pad | solution.py:78
  436.5 18.6 %pad.110 = f32[64,16,1024]{2,1,0:T(8,128)} pad(f32[32,16,1024]{2,1,0:T(8,128)} %pad_maximum_fusion.3, f32[]{:T(128)} %constant.13.clone.1), padding=0_1_1x0_0_0x0_0_0 | pad | bytes 6291460 | tf_op jit(solution)/shard_map/pad | solution.py:78
  455.1 11.9 %pad.111 = f32[64,16,1024]{2,1,0:T(8,128)} pad(f32[32,16,1024]{2,1,0:T(8,128)S(1)} %copy-done.15, f32[]{:T(128)} %constant.13.clone.1), padding=1_0_1x0_0_0x0_0_0 | pad | bytes 6291460 | tf_op jit(solution)/shard_map/pad | solution.py:78
  467.0 7.1 add.265
  475.6 7.6 fusion.12
  485.7 35.5 %pad.98 = f32[128,16,1024]{2,1,0:T(8,128)} pad(f32[64,16,1024]{2,1,0:T(8,128)} %pad_maximum_fusion, f32[]{:T(128)} %constant.13.clone.1), padding=0_1_1x0_0_0x0_0_0 | pad | bytes 12582916 | tf_op jit(solution)/shard_map/pad | solution.py:78
  521.2 35.5 %pad.113 = f32[128,16,1024]{2,1,0:T(8,128)} pad(f32[64,16,1024]{2,1,0:T(8,128)} %add.265, f32[]{:T(128)} %constant.13.clone.1), padding=1_0_1x0_0_0x0_0_0 | pad | bytes 12582916 | tf_op jit(solution)/shard_map/pad | solution.py:78
  556.8 4.8 pad_maximum_fusion.1
  561.5 35.5 %pad.112 = f32[128,16,1024]{2,1,0:T(8,128)} pad(f32[64,16,1024]{2,1,0:T(8,128)} %pad_maximum_fusion.1, f32[]{:T(128)} %constant.13.clone.1), padding=0_1_1x0_0_0x0_0_0 | pad | bytes 12582916 | tf_op jit(solution)/shard_map/pad | solution.py:78
  598.8 107.7 %while.11 = (s32[]{:T(128)}, f32[16,1024]{1,0:T(8,128)S(1)}, f32[16,1024]{1,0:T(8,128)S(1)}, f32[16,1024]{1,0:T(8,128)S(1)}, s32[]{:T(128)}, /*index=5*/s32[]{:T(128)}) while((s32[]{:T(128)}, f32[16,1024]{1,0:T(8,128)S(1)}, f32[16,1024]{1,0:T(8,128)S(1)}, f32[16,1024]{1,0:T(8,128)S(1)}, s32[]{:T(128)}, /*index=5*/s32[]{:T(128)}) %tuple.47), condition=%wide.region_4.5_spmd.clone, body=%wide.region_3.4_spmd.clone.sunk | while | flops 81923 | bytes 458871 | solution.py:87
  603.9 4.2 collective-permute-start
  609.7 4.3 collective-permute-start
  621.5 4.2 collective-permute-start
  627.3 5.6 collective-permute-start
  634.5 6.5 collective-permute-start
  642.6 6.5 collective-permute-start
  650.7 6.3 collective-permute-start
  658.6 6.3 collective-permute-start
  666.6 6.3 collective-permute-start
  674.6 6.2 collective-permute-start
  682.5 6.3 collective-permute-start
  690.4 6.5 collective-permute-start
  698.5 6.3 collective-permute-start
  706.5 14.0 %multiply_reduce_fusion = f32[128,1024]{1,0:T(8,128)S(1)} fusion(f32[128,16,1024]{2,1,0:T(8,128)} %pad.112, f32[128,16,1024]{2,1,0:T(8,128)} %pad.113, f32[128,16,1024]{2,1,0:T(8,128)} %pad.98, f32[128,16,1024]{2,1,0:T(8,128)} %pad.99, f32[16,1024]{1,0:T(8,128)S(1)} %get-tuple-element.27, f32[128,16]{1,0:T(8,128)S(1)} %copy-done.28), kind=kLoop, calls=%fused_computation.3 | loop fusion | flops 12451840 | bytes 34152448 | tf_op jit(solution)/shard_map/reduce_sum | solution.py:89
  720.5 5.7 convolution_convert_fusion
  727.1 39.7 %reduce-scatter.3.cloned.1.call-done = bf16[16,4096]{1,0:T(8,128)(2,1)} async-done(((bf16[128,4096]{1,0:T(8,128)(2,1)}), bf16[16,4096]{1,0:T(8,128)(2,1)}) %reduce-scatter.3.cloned.1.call-update) | async-done | bytes 131088 | tf_op jit(solution)/shard_map/reduce_scatter | solution.py:96
  769.3 16.9 %all_to_all.10 = bf16[16,4,4096]{2,1,0:T(4,128)(2,1)S(1)} all-to-all(bf16[16,4,4096]{2,1,0:T(4,128)(2,1)S(1)} %reshape.78), channel_id=1, replica_groups=mesh['seq'=16,'expert'=8] {'seq'}, dimensions={0} | all-to-all | bytes 1048576 | tf_op jit(solution)/shard_map/all_to_all | solution.py:113
  787.2 29.3 %all-gather.11.cloned.1.call-done = bf16[8,64,4096]{2,1,0:T(8,128)(2,1)} async-done(((bf16[1,64,4096]{2,1,0:T(8,128)(2,1)}), bf16[8,64,4096]{2,1,0:T(8,128)(2,1)}) %all-gather.11.cloned.1.call-update) | async-done | bytes 4194320 | tf_op jit(solution)/shard_map/all_gather | solution.py:116
  816.5 10.1 %fusion.6 = f32[512,896]{1,0:T(8,128)} fusion(bf16[512,4096]{1,0:T(8,128)(2,1)} %bitcast.51, bf16[1,4096,896]{2,1,0:T(8,128)(2,1)} %param.33), kind=kOutput, calls=%fused_computation.9 | convolution fusion | flops 3758096384 | bytes 13369344 | tf_op jit(solution)/shard_map/dot_general | solution.py:119
  826.6 16.7 %fusion.8 = bf16[512,4096]{1,0:T(8,128)(2,1)} fusion(bf16[1,896,4096]{2,1,0:T(8,128)(2,1)} %param.35, f32[512,896]{1,0:T(8,128)} %fusion.6, bf16[512,4096]{1,0:T(8,128)(2,1)} %bitcast.52, bf16[1,4096,896]{2,1,0:T(8,128)(2,1)} %param.34), kind=kOutput, calls=%fused_computation.11 | convolution fusion | flops 7521042432 | bytes 24903680 | tf_op jit(solution)/shard_map/dot_general | solution.py:123
  843.3 38.0 %reduce-scatter.5.cloned.1.call-done = bf16[64,4096]{1,0:T(8,128)(2,1)} async-done(((bf16[512,4096]{1,0:T(8,128)(2,1)}), bf16[64,4096]{1,0:T(8,128)(2,1)}) %reduce-scatter.5.cloned.1.call-update) | async-done | bytes 524304 | tf_op jit(solution)/shard_map/reduce_scatter | solution.py:122
  883.3 7.1 all-to-all-start.1
  890.5 10.1 %all-to-all-done.1 = bf16[16,4,4096]{2,1,0:T(4,128)(2,1)S(1)} async-done(((bf16[16,4,4096]{2,1,0:T(4,128)(2,1)}), bf16[16,4,4096]{2,1,0:T(4,128)(2,1)S(1)}, u32[]{:S(2)}, u32[]{:S(2)}) %all-to-all-start.1) | async-done | bytes 524320 | tf_op jit(solution)/shard_map/all_to_all | solution.py:128
  (241 shorter events, 138.8 us)
Async XLA Ops:
  6.5 155.7 %copy-start = (bf16[1024,288]{0,1:T(8,128)(2,1)S(1)}, bf16[1024,288]{0,1:T(8,128)(2,1)}, u32[]{:S(2)}) copy-start(bf16[1024,288]{0,1:T(8,128)(2,1)} %param.24) | copy-start | bytes 1769476
  6.5 28.4 %all-gather.5.cloned.1.call-start = ((), (), s32[]{:S(2)}) async-start(), calls=%async_computation.4 | async-start | bytes 1179648 | tf_op jit(solution)/shard_map/all_gather | solution.py:49
  7.3 141.1 %all-gather.7.cloned.1.call-start = ((), (), s32[]{:S(2)}) async-start(), calls=%async_computation.5 | async-start | bytes 17825792 | tf_op jit(solution)/shard_map/all_gather | solution.py:55
  8.0 215.6 %all-reduce.30.cloned.1.call-start = ((), (), s32[]{:S(2)}) async-start(), calls=%async_computation.6 | async-start | bytes 131072 | tf_op jit(solution)/shard_map/psum | solution.py:68
  36.4 125.5 %copy-start.39 = (f32[1024]{0:T(1024)S(1)}, f32[1024]{0:T(1024)}, u32[]{:S(2)}) copy-start(f32[1024]{0:T(1024)} %param.23) | copy-start | bytes 12292
  36.4 187.1 %copy-start.42 = (bf16[256,1024]{1,0:T(8,128)(2,1)S(1)}, bf16[256,1024]{1,0:T(8,128)(2,1)}, u32[]{:S(2)}) copy-start(bf16[256,1024]{1,0:T(8,128)(2,1)} %param.25) | copy-start | bytes 1572868
  36.4 187.1 %copy-start.43 = (f32[1024]{0:T(1024)S(1)}, f32[1024]{0:T(1024)}, u32[]{:S(2)}) copy-start(f32[1024]{0:T(1024)} %param.26) | copy-start | bytes 12292
  156.9 68.0 %copy-start.37 = (f32[16,1024]{1,0:T(8,128)S(1)}, f32[16,1024]{1,0:T(8,128)}, u32[]{:S(2)}) copy-start(f32[16,1024]{1,0:T(8,128)} %param.27) | copy-start | bytes 196612
  156.9 5.0 collective-permute-start.1
  162.2 64.8 %copy-start.23 = (bf16[128,1024]{1,0:T(8,128)(2,1)}, bf16[128,1024]{1,0:T(8,128)(2,1)S(1)}, u32[]{:S(2)}) copy-start(bf16[128,1024]{1,0:T(8,128)(2,1)S(1)} %multiply_convert_fusion.1) | copy-start | bytes 786436
  163.2 557.3 %all-gather.9.cloned.1.call-start = ((), (), s32[]{:S(2)}) async-start(), calls=%async_computation.7 | async-start | bytes 8912896 | tf_op jit(solution)/shard_map/all_gather | solution.py:93
  163.8 602.9 %reduce-scatter.3.cloned.1.call-start = ((), (), s32[]{:S(2)}) async-start(), calls=%async_computation.8 | async-start | bytes 1179648 | tf_op jit(solution)/shard_map/reduce_scatter | solution.py:96
  280.3 8.2 copy-start.36
  288.5 8.3 copy-start.20
  308.4 27.3 %copy-start.33 = (f32[1,16,1024]{2,1,0:T(8,128)S(1)}, f32[1,16,1024]{2,1,0:T(8,128)}, u32[]{:S(2)}) copy-start(f32[1,16,1024]{2,1,0:T(8,128)} %slice.347) | copy-start | bytes 196612
  362.0 18.6 %copy-start.16 = (f32[32,16,1024]{2,1,0:T(8,128)S(1)}, f32[32,16,1024]{2,1,0:T(8,128)}, u32[]{:S(2)}) copy-start(f32[32,16,1024]{2,1,0:T(8,128)} %add.255) | copy-start | bytes 6291460
  399.4 35.6 %copy-start.17 = (f32[31,16,1024]{2,1,0:T(8,128)S(1)}, f32[31,16,1024]{2,1,0:T(8,128)}, u32[]{:S(2)}) copy-start(f32[31,16,1024]{2,1,0:T(8,128)} %get-tuple-element.56) | copy-start | bytes 6094852
  399.4 35.6 %copy-start.31 = (f32[1,16,1024]{2,1,0:T(8,128)S(1)}, f32[1,16,1024]{2,1,0:T(8,128)}, u32[]{:S(2)}) copy-start(f32[1,16,1024]{2,1,0:T(8,128)} %slice.369) | copy-start | bytes 196612
  436.5 18.6 %copy-start.15 = (f32[32,16,1024]{2,1,0:T(8,128)S(1)}, f32[32,16,1024]{2,1,0:T(8,128)}, u32[]{:S(2)}) copy-start(f32[32,16,1024]{2,1,0:T(8,128)} %add.264) | copy-start | bytes 6291460
  467.0 8.6 copy-start.6
  521.2 35.5 %copy-start.29 = (f32[1,16,1024]{2,1,0:T(8,128)S(1)}, f32[1,16,1024]{2,1,0:T(8,128)}, u32[]{:S(2)}) copy-start(f32[1,16,1024]{2,1,0:T(8,128)} %slice.368) | copy-start | bytes 196612
  561.5 144.9 %copy-start.28 = (f32[128,16]{1,0:T(8,128)S(1)}, f32[128,16]{1,0:T(8,128)}, u32[]{:S(2)}) copy-start(f32[128,16]{1,0:T(8,128)} %copy.42) | copy-start | bytes 24580
  598.8 5.0 collective-permute-start
  603.9 5.8 collective-permute-start
  609.7 5.9 collective-permute-start
  615.6 5.8 collective-permute-start
  621.5 5.8 collective-permute-start
  627.3 7.2 collective-permute-start
  634.5 8.1 collective-permute-start
  642.6 8.1 collective-permute-start
  650.7 7.9 collective-permute-start
  658.6 7.9 collective-permute-start
  666.6 8.0 collective-permute-start
  674.6 7.8 collective-permute-start
  682.5 7.9 collective-permute-start
  690.4 8.1 collective-permute-start
  698.5 7.9 collective-permute-start
  706.5 14.1 %copy-start.19 = (f32[128,2,1024]{2,0,1:T(8,128)S(1)}, f32[128,2,1024]{2,0,1:T(8,128)}, u32[]{:S(2)}) copy-start(f32[128,2,1024]{2,0,1:T(8,128)} %copy-done.18) | copy-start | bytes 3145732
  706.5 14.1 %copy-start.24 = (bf16[128,1024]{1,0:T(8,128)(2,1)S(1)}, bf16[128,1024]{1,0:T(8,128)(2,1)}, u32[]{:S(2)}) copy-start(bf16[128,1024]{1,0:T(8,128)(2,1)} %copy-done.23) | copy-start | bytes 786436
  706.5 14.1 %copy-start.44 = (f32[1024]{0:T(1024)S(1)}, f32[1024]{0:T(1024)}, u32[]{:S(2)}) copy-start(f32[1024]{0:T(1024)} %param.28) | copy-start | bytes 12292
  720.5 46.3 %copy-start.21 = (bf16[16,4096]{1,0:T(8,128)(2,1)S(1)}, bf16[16,4096]{1,0:T(8,128)(2,1)}, u32[]{:S(2)}) copy-start(bf16[16,4096]{1,0:T(8,128)(2,1)} %param.19) | copy-start | bytes 393220
  720.5 47.3 %copy-start.38 = (f32[4096]{0:T(1024)S(1)}, f32[4096]{0:T(1024)}, u32[]{:S(2)}) copy-start(f32[4096]{0:T(1024)} %param.30) | copy-start | bytes 49156
  726.3 90.2 %all-gather.11.cloned.1.call-start = ((), (), s32[]{:S(2)}) async-start(), calls=%async_computation.9 | async-start | bytes 4718592 | tf_op jit(solution)/shard_map/all_gather | solution.py:116
  787.1 94.2 %reduce-scatter.5.cloned.1.call-start = ((), (), s32[]{:S(2)}) async-start(), calls=%async_computation.10 | async-start | bytes 4718592 | tf_op jit(solution)/shard_map/reduce_scatter | solution.py:122
  826.6 75.1 %copy-start.1 = (bf16[1024,288]{0,1:T(8,128)(2,1)S(1)}, bf16[1024,288]{0,1:T(8,128)(2,1)}, u32[]{:S(2)}) copy-start(bf16[1024,288]{0,1:T(8,128)(2,1)} %param.24) | copy-start | bytes 1769476
  843.2 47.2 %copy-start.41 = (f32[16,2]{0,1:T(2,128)S(1)}, f32[16,2]{0,1:T(2,128)}, u32[]{:S(2)}) copy-start(f32[16,2]{0,1:T(2,128)} %param.32) | copy-start | bytes 388
  843.2 57.4 %copy-start.22 = (bf16[16,4096]{1,0:T(8,128)(2,1)S(1)}, bf16[16,4096]{1,0:T(8,128)(2,1)}, u32[]{:S(2)}) copy-start(bf16[16,4096]{1,0:T(8,128)(2,1)} %reduce-scatter.3.cloned.1.call-done) | copy-start | bytes 393220
  883.3 17.2 %all-to-all-start.1 = ((bf16[16,4,4096]{2,1,0:T(4,128)(2,1)}), bf16[16,4,4096]{2,1,0:T(4,128)(2,1)S(1)}, u32[]{:S(2)}, u32[]{:S(2)}) async-start(bf16[16,4,4096]{2,1,0:T(4,128)(2,1)} %reshape.81), calls=%async_computation.3 | async-start | bytes 1048576 | tf_op jit(solution)/shard_map/all_to_all | solution.py:128
  (21 other events, 86.6 us)
Sparse Core Ops, SparseCore 0:
  9.1 25.7 all-gather.4
  37.0 111.3 all-gather.6
  163.4 60.1 all-reduce.29
  225.7 77.5 all-gather.8
  726.4 40.3 reduce-scatter.2
  787.2 29.2 all-gather.10
  843.4 37.8 reduce-scatter.4
where the time goes:
time: 924 us; the launch traced here: 909 us
  waiting for transfers between devices  327 us (35%)
  local copies, waits for them, and re-layouts  289 us (31%)
  other arithmetic  109 us (12%)
  starting transfers between devices  94.2 us (10%)
  matrix products  44.8 us (5%)
  blocking collectives  30.9 us (3%)
  between operations  14 us (2%)
    pad x24, local copies, waits for them, and re-layouts, per_device(): lax.associative_scan(combine_states, (decay, source), axis=0)  267 us
    all_gather x1, waiting for transfers between devices, per_device(): lax.all_gather(in_weight, 'seq', axis=1, tiled=True)  112 us
    ppermute x16, starting transfers between devices, from_behind(): return lax.ppermute(block, axis, route)  86.9 us
    psum x1, waiting for transfers between devices, per_device(): lax.psum(partial_value[:, :RANK].astype(jnp.bfloat16), 'expert')  44.8 us
    reduce_scatter x1, waiting for transfers between devices, per_device(): lax.psum_scatter(terms.astype(jnp.bfloat16), 'expert', scatter_dimension=...  39.7 us
    reduce_scatter x1, waiting for transfers between devices, per_device(): lax.psum_scatter(jnp.dot(act, w_down[0], preferred_element_type=jnp.float...  38 us
    add x12, other arithmetic, combine_states(): return (earlier[0] * later[0], later[0] * earlier[1] + later[1])  34.6 us
    add x12, other arithmetic, per_device(): lax.associative_scan(combine_states, (decay, source), axis=0)  33.2 us
  transfers between devices with their start and end apart: 24, of which 23 were waited for; matrix products, arithmetic and copies ran while one was open for 42% of the time, Pallas kernels for 0%

commit v1 on v0

--- a/solution.py
+++ b/solution.py
@@ -52,7 +52,9 @@
     both = jnp.einsum(
         "td,kdc->tkc",
         normed,
-        lax.all_gather(in_weight, "seq", axis=1, tiled=True),
+        jnp.concatenate(
+            lax.all_to_all(jnp.stack([in_weight] * lax.axis_size("seq")), "seq", 0, 0), axis=1
+        ),
         preferred_element_type=jnp.float32,
     )
     xpart = both[:, 0]

time: 924 us -> 1050 us (1.14)
  waiting for transfers between devices: 327 us -> 438 us
  local copies, waits for them, and re-layouts: 289 us -> 303 us
    all_to_all x0 -> x1, waiting for transfers between devices: none -> 221 us  [per_device(): lax.all_to_all(jnp.stack([in_weight] * lax.axis_size('seq')), 'seq', 0, 0)]
    all_gather x1 -> x0, waiting for transfers between devices: 112 us -> none  [per_device(): lax.all_gather(in_weight, 'seq', axis=1, tiled=True)]
  transfers between devices with their start and end apart: 24 -> 24, of which waited for: 23 -> 23; matrix products, arithmetic and copies ran while one was open for 42% -> 37% of each run, Pallas kernels for 0% -> 0%
where the time goes in v1:
time: 1050 us; the launch traced here: 1030 us
  waiting for transfers between devices  438 us (42%)
  local copies, waits for them, and re-layouts  303 us (29%)
  other arithmetic  108 us (10%)
  starting transfers between devices  99.7 us (9%)
  matrix products  38.8 us (4%)
  blocking collectives  30.1 us (3%)
  between operations  15.2 us (1%)
    pad x24, local copies, waits for them, and re-layouts, per_device(): lax.associative_scan(combine_states, (decay, source), axis=0)  267 us
    all_to_all x1, waiting for transfers between devices, per_device(): lax.all_to_all(jnp.stack([in_weight] * lax.axis_size('seq')), 'seq', 0, 0)  221 us
    ppermute x16, starting transfers between devices, from_behind(): return lax.ppermute(block, axis, route)  84.1 us
    psum x1, waiting for transfers between devices, per_device(): lax.psum(partial_value[:, :RANK].astype(jnp.bfloat16), 'expert')  47.5 us
    reduce_scatter x1, waiting for transfers between devices, per_device(): lax.psum_scatter(terms.astype(jnp.bfloat16), 'expert', scatter_dimension=...  39.7 us
    reduce_scatter x1, waiting for transfers between devices, per_device(): lax.psum_scatter(jnp.dot(act, w_down[0], preferred_element_type=jnp.float...  37.9 us
    add x12, other arithmetic, combine_states(): return (earlier[0] * later[0], later[0] * earlier[1] + later[1])  34.2 us
    add x12, other arithmetic, per_device(): lax.associative_scan(combine_states, (decay, source), axis=0)  33.1 us
  transfers between devices with their start and end apart: 24, of which 23 were waited for; matrix products, arithmetic and copies ran while one was open for 37% of the time, Pallas kernels for 0%

profile of v1, /device:TPU:0, one launch (start us, length us, event | category | flops | bytes accessed | tf_op | source)
XLA Modules:
  0.0 1034.3 jit_solution(18035692133829836670)
XLA Ops:
  7.4 6.9 stack.2
  14.3 8.3 all-to-all-start
  23.4 26.6 %all-gather.4.cloned.1.call-done = bf16[128,4096]{1,0:T(8,128)(2,1)} async-done(((bf16[16,4096]{1,0:T(8,128)(2,1)}), bf16[128,4096]{1,0:T(8,128)(2,1)}) %all-gather.4.cloned.1.call-update) | async-done | bytes 1048592 | tf_op jit(solution)/shard_map/all_gather | solution.py:49
  51.6 220.8 %all-to-all-done = bf16[16,2,256,1024]{3,2,1,0:T(8,128)(2,1)} async-done(((bf16[16,2,256,1024]{3,2,1,0:T(8,128)(2,1)}), bf16[16,2,256,1024]{3,2,1,0:T(8,128)(2,1)}, u32[]{:S(2)}, u32[]{:S(2)}) %all-to-all-start) | async-done | bytes 16777248 | tf_op jit(solution)/shard_map/all_to_all | solution.py:56
  272.4 8.3 copy.44
  288.0 13.2 %psum.14 = bf16[128,32]{0,1:T(8,128)(2,1)S(1)} all-reduce(bf16[128,32]{0,1:T(8,128)(2,1)S(1)} %slice.341), channel_id=1, replica_groups=mesh['seq'=16,'expert'=8] {'expert'}, use_global_device_ids=true, to_apply=%region_1.2 | all-reduce | flops 4096 | bytes 16384 | tf_op jit(solution)/shard_map/psum | solution.py:71
  302.0 47.5 %all-reduce.30.cloned.1.call-done = bf16[128,256]{0,1:T(8,128)(2,1)} async-done(((bf16[128,256]{0,1:T(8,128)(2,1)}), bf16[128,256]{0,1:T(8,128)(2,1)}) %all-reduce.30.cloned.1.call-update) | async-done | bytes 65552 | tf_op jit(solution)/shard_map/psum | solution.py:70
  359.6 10.8 %slice_add_fusion = (f32[64,16,1024]{2,1,0:T(8,128)S(1)}, f32[64,16,1024]{2,1,0:T(8,128)}) fusion(f32[128,16,1024]{2,1,0:T(8,128)} %copy-done.3, f32[128,16,1024]{2,1,0:T(8,128)} %copy-done.2), kind=kLoop, calls=%fused_computation.19 | loop fusion | flops 3145728 | bytes 25165824 | tf_op jit(solution)/shard_map/add | solution.py:24
  434.3 7.0 pad.108
  441.3 10.2 pad.109
  451.4 10.1 pad.95
  463.9 10.2 pad.94
  474.0 4.2 add.255
  481.3 5.0 fusion.16
  487.9 18.6 %pad.96 = f32[64,16,1024]{2,1,0:T(8,128)} pad(f32[32,16,1024]{2,1,0:T(8,128)} %pad_maximum_fusion.2, f32[]{:T(128)} %constant.13.clone.1), padding=0_1_1x0_0_0x0_0_0 | pad | bytes 6291460 | tf_op jit(solution)/shard_map/pad | solution.py:80
  506.6 12.0 %pad.97 = f32[64,16,1024]{2,1,0:T(8,128)} pad(f32[32,16,1024]{2,1,0:T(8,128)S(1)} %copy-done.16, f32[]{:T(128)} %constant.13.clone.1), padding=1_0_1x0_0_0x0_0_0 | pad | bytes 6291460 | tf_op jit(solution)/shard_map/pad | solution.py:80
  518.6 6.8 add.257
  525.4 35.6 %pad.99 = f32[128,16,1024]{2,1,0:T(8,128)} pad(f32[64,16,1024]{2,1,0:T(8,128)} %add.257, f32[]{:T(128)} %constant.13.clone.1), padding=1_0_1x0_0_0x0_0_0 | pad | bytes 12582916 | tf_op jit(solution)/shard_map/pad | solution.py:80
  562.5 18.6 %pad.110 = f32[64,16,1024]{2,1,0:T(8,128)} pad(f32[32,16,1024]{2,1,0:T(8,128)} %pad_maximum_fusion.3, f32[]{:T(128)} %constant.13.clone.1), padding=0_1_1x0_0_0x0_0_0 | pad | bytes 6291460 | tf_op jit(solution)/shard_map/pad | solution.py:80
  581.1 12.0 %pad.111 = f32[64,16,1024]{2,1,0:T(8,128)} pad(f32[32,16,1024]{2,1,0:T(8,128)S(1)} %copy-done.15, f32[]{:T(128)} %constant.13.clone.1), padding=1_0_1x0_0_0x0_0_0 | pad | bytes 6291460 | tf_op jit(solution)/shard_map/pad | solution.py:80
  593.1 7.1 add.265
  601.7 7.4 fusion.12
  611.7 35.6 %pad.98 = f32[128,16,1024]{2,1,0:T(8,128)} pad(f32[64,16,1024]{2,1,0:T(8,128)} %pad_maximum_fusion, f32[]{:T(128)} %constant.13.clone.1), padding=0_1_1x0_0_0x0_0_0 | pad | bytes 12582916 | tf_op jit(solution)/shard_map/pad | solution.py:80
  647.3 35.6 %pad.113 = f32[128,16,1024]{2,1,0:T(8,128)} pad(f32[64,16,1024]{2,1,0:T(8,128)} %add.265, f32[]{:T(128)} %constant.13.clone.1), padding=1_0_1x0_0_0x0_0_0 | pad | bytes 12582916 | tf_op jit(solution)/shard_map/pad | solution.py:80
  682.8 4.8 pad_maximum_fusion.1
  687.6 35.6 %pad.112 = f32[128,16,1024]{2,1,0:T(8,128)} pad(f32[64,16,1024]{2,1,0:T(8,128)} %pad_maximum_fusion.1, f32[]{:T(128)} %constant.13.clone.1), padding=0_1_1x0_0_0x0_0_0 | pad | bytes 12582916 | tf_op jit(solution)/shard_map/pad | solution.py:80
  724.9 107.1 %while.11 = (s32[]{:T(128)}, f32[16,1024]{1,0:T(8,128)S(1)}, f32[16,1024]{1,0:T(8,128)S(1)}, f32[16,1024]{1,0:T(8,128)S(1)}, s32[]{:T(128)}, /*index=5*/s32[]{:T(128)}) while((s32[]{:T(128)}, f32[16,1024]{1,0:T(8,128)S(1)}, f32[16,1024]{1,0:T(8,128)S(1)}, f32[16,1024]{1,0:T(8,128)S(1)}, s32[]{:T(128)}, /*index=5*/s32[]{:T(128)}) %tuple.47), condition=%wide.region_4.5_spmd.clone, body=%wide.region_3.4_spmd.clone.sunk | while | flops 81923 | bytes 458871 | solution.py:89
  735.9 4.4 collective-permute-start
  753.5 5.1 collective-permute-start
  760.3 6.3 collective-permute-start
  768.2 6.5 collective-permute-start
  776.3 6.3 collective-permute-start
  784.2 6.3 collective-permute-start
  792.2 6.3 collective-permute-start
  800.2 6.2 collective-permute-start
  808.1 6.3 collective-permute-start
  816.0 6.5 collective-permute-start
  824.1 6.3 collective-permute-start
  832.1 14.0 %multiply_reduce_fusion = f32[128,1024]{1,0:T(8,128)S(1)} fusion(f32[128,16,1024]{2,1,0:T(8,128)} %pad.112, f32[128,16,1024]{2,1,0:T(8,128)} %pad.113, f32[128,16,1024]{2,1,0:T(8,128)} %pad.98, f32[128,16,1024]{2,1,0:T(8,128)} %pad.99, f32[16,1024]{1,0:T(8,128)S(1)} %get-tuple-element.27, f32[128,16]{1,0:T(8,128)S(1)} %copy-done.29), kind=kLoop, calls=%fused_computation.3 | loop fusion | flops 12451840 | bytes 34152448 | tf_op jit(solution)/shard_map/reduce_sum | solution.py:91
  846.1 5.7 convolution_convert_fusion
  852.7 39.7 %reduce-scatter.3.cloned.1.call-done = bf16[16,4096]{1,0:T(8,128)(2,1)} async-done(((bf16[128,4096]{1,0:T(8,128)(2,1)}), bf16[16,4096]{1,0:T(8,128)(2,1)}) %reduce-scatter.3.cloned.1.call-update) | async-done | bytes 131088 | tf_op jit(solution)/shard_map/reduce_scatter | solution.py:98
  894.9 17.0 %all_to_all.15 = bf16[16,4,4096]{2,1,0:T(4,128)(2,1)S(1)} all-to-all(bf16[16,4,4096]{2,1,0:T(4,128)(2,1)S(1)} %reshape.88), channel_id=1, replica_groups=mesh['seq'=16,'expert'=8] {'seq'}, dimensions={0} | all-to-all | bytes 1048576 | tf_op jit(solution)/shard_map/all_to_all | solution.py:115
  912.9 29.3 %all-gather.8.cloned.1.call-done = bf16[8,64,4096]{2,1,0:T(8,128)(2,1)} async-done(((bf16[1,64,4096]{2,1,0:T(8,128)(2,1)}), bf16[8,64,4096]{2,1,0:T(8,128)(2,1)}) %all-gather.8.cloned.1.call-update) | async-done | bytes 4194320 | tf_op jit(solution)/shard_map/all_gather | solution.py:118
  942.2 10.1 fusion.6
  952.3 16.6 %fusion.8 = bf16[512,4096]{1,0:T(8,128)(2,1)} fusion(bf16[1,896,4096]{2,1,0:T(8,128)(2,1)} %param.35, f32[512,896]{1,0:T(8,128)} %fusion.6, bf16[512,4096]{1,0:T(8,128)(2,1)} %bitcast.55, bf16[1,4096,896]{2,1,0:T(8,128)(2,1)} %param.34), kind=kOutput, calls=%fused_computation.11 | convolution fusion | flops 7521042432 | bytes 24903680 | tf_op jit(solution)/shard_map/dot_general | solution.py:125
  969.0 37.9 %reduce-scatter.5.cloned.1.call-done = bf16[64,4096]{1,0:T(8,128)(2,1)} async-done(((bf16[512,4096]{1,0:T(8,128)(2,1)}), bf16[64,4096]{1,0:T(8,128)(2,1)}) %reduce-scatter.5.cloned.1.call-update) | async-done | bytes 524304 | tf_op jit(solution)/shard_map/reduce_scatter | solution.py:124
  1009.0 7.0 all-to-all-start.2
  1016.0 10.1 all-to-all-done.2
  (248 shorter events, 146.1 us)
Async XLA Ops:
  7.4 279.0 %copy-start = (bf16[1024,288]{0,1:T(8,128)(2,1)S(1)}, bf16[1024,288]{0,1:T(8,128)(2,1)}, u32[]{:S(2)}) copy-start(bf16[1024,288]{0,1:T(8,128)(2,1)} %param.24) | copy-start | bytes 1769476
  14.3 9.1 copy-start.41
  14.3 258.0 %all-to-all-start = ((bf16[16,2,256,1024]{3,2,1,0:T(8,128)(2,1)}), bf16[16,2,256,1024]{3,2,1,0:T(8,128)(2,1)}, u32[]{:S(2)}, u32[]{:S(2)}) async-start(bf16[16,2,256,1024]{3,2,1,0:T(8,128)(2,1)} %stack.2), calls=%async_computation | async-start | bytes 33554432 | tf_op jit(solution)/shard_map/all_to_all | solution.py:56
  22.6 27.4 %all-gather.4.cloned.1.call-start = ((), (), s32[]{:S(2)}) async-start(), calls=%async_computation.5 | async-start | bytes 1179648 | tf_op jit(solution)/shard_map/all_gather | solution.py:49
  23.4 326.2 %all-reduce.30.cloned.1.call-start = ((), (), s32[]{:S(2)}) async-start(), calls=%async_computation.6 | async-start | bytes 131072 | tf_op jit(solution)/shard_map/psum | solution.py:70
  272.3 8.3 copy-start.20
  272.4 8.3 copy-start.39
  280.6 68.9 %copy-start.45 = (bf16[256,1024]{1,0:T(8,128)(2,1)S(1)}, bf16[256,1024]{1,0:T(8,128)(2,1)}, u32[]{:S(2)}) copy-start(bf16[256,1024]{1,0:T(8,128)(2,1)} %param.25) | copy-start | bytes 1572868
  280.7 68.9 %copy-start.46 = (f32[1024]{0:T(1024)S(1)}, f32[1024]{0:T(1024)}, u32[]{:S(2)}) copy-start(f32[1024]{0:T(1024)} %param.26) | copy-start | bytes 12292
  283.1 67.8 %copy-start.38 = (f32[16,1024]{1,0:T(8,128)S(1)}, f32[16,1024]{1,0:T(8,128)}, u32[]{:S(2)}) copy-start(f32[16,1024]{1,0:T(8,128)} %param.27) | copy-start | bytes 196612
  283.2 2.9 collective-permute-start.1
  286.4 66.6 %copy-start.24 = (bf16[128,1024]{1,0:T(8,128)(2,1)}, bf16[128,1024]{1,0:T(8,128)(2,1)S(1)}, u32[]{:S(2)}) copy-start(bf16[128,1024]{1,0:T(8,128)(2,1)S(1)} %multiply_convert_fusion.1) | copy-start | bytes 786436
  287.4 558.7 %all-gather.6.cloned.1.call-start = ((), (), s32[]{:S(2)}) async-start(), calls=%async_computation.7 | async-start | bytes 8912896 | tf_op jit(solution)/shard_map/all_gather | solution.py:95
  288.0 604.4 %reduce-scatter.3.cloned.1.call-start = ((), (), s32[]{:S(2)}) async-start(), calls=%async_computation.8 | async-start | bytes 1179648 | tf_op jit(solution)/shard_map/reduce_scatter | solution.py:98
  434.3 27.3 %copy-start.34 = (f32[1,16,1024]{2,1,0:T(8,128)S(1)}, f32[1,16,1024]{2,1,0:T(8,128)}, u32[]{:S(2)}) copy-start(f32[1,16,1024]{2,1,0:T(8,128)} %slice.347) | copy-start | bytes 196612
  487.9 18.7 %copy-start.16 = (f32[32,16,1024]{2,1,0:T(8,128)S(1)}, f32[32,16,1024]{2,1,0:T(8,128)}, u32[]{:S(2)}) copy-start(f32[32,16,1024]{2,1,0:T(8,128)} %add.255) | copy-start | bytes 6291460
  525.4 35.6 %copy-start.17 = (f32[31,16,1024]{2,1,0:T(8,128)S(1)}, f32[31,16,1024]{2,1,0:T(8,128)}, u32[]{:S(2)}) copy-start(f32[31,16,1024]{2,1,0:T(8,128)} %get-tuple-element.56) | copy-start | bytes 6094852
  525.4 35.6 %copy-start.32 = (f32[1,16,1024]{2,1,0:T(8,128)S(1)}, f32[1,16,1024]{2,1,0:T(8,128)}, u32[]{:S(2)}) copy-start(f32[1,16,1024]{2,1,0:T(8,128)} %slice.369) | copy-start | bytes 196612
  562.5 18.6 %copy-start.15 = (f32[32,16,1024]{2,1,0:T(8,128)S(1)}, f32[32,16,1024]{2,1,0:T(8,128)}, u32[]{:S(2)}) copy-start(f32[32,16,1024]{2,1,0:T(8,128)} %add.264) | copy-start | bytes 6291460
  593.1 8.6 copy-start.6
  647.3 35.6 %copy-start.30 = (f32[1,16,1024]{2,1,0:T(8,128)S(1)}, f32[1,16,1024]{2,1,0:T(8,128)}, u32[]{:S(2)}) copy-start(f32[1,16,1024]{2,1,0:T(8,128)} %slice.368) | copy-start | bytes 196612
  687.6 144.4 %copy-start.29 = (f32[128,16]{1,0:T(8,128)S(1)}, f32[128,16]{1,0:T(8,128)}, u32[]{:S(2)}) copy-start(f32[128,16]{1,0:T(8,128)} %copy.45) | copy-start | bytes 24580
  725.0 4.9 collective-permute-start
  729.9 5.9 collective-permute-start
  735.9 6.0 collective-permute-start
  741.9 5.8 collective-permute-start
  747.7 5.8 collective-permute-start
  753.5 6.7 collective-permute-start
  760.3 7.9 collective-permute-start
  768.2 8.1 collective-permute-start
  776.3 7.9 collective-permute-start
  784.2 7.9 collective-permute-start
  792.2 8.0 collective-permute-start
  800.2 7.8 collective-permute-start
  808.1 7.9 collective-permute-start
  816.0 8.1 collective-permute-start
  824.1 7.9 collective-permute-start
  832.0 14.1 %copy-start.19 = (f32[128,2,1024]{2,0,1:T(8,128)S(1)}, f32[128,2,1024]{2,0,1:T(8,128)}, u32[]{:S(2)}) copy-start(f32[128,2,1024]{2,0,1:T(8,128)} %copy-done.18) | copy-start | bytes 3145732
  832.1 14.1 %copy-start.25 = (bf16[128,1024]{1,0:T(8,128)(2,1)S(1)}, bf16[128,1024]{1,0:T(8,128)(2,1)}, u32[]{:S(2)}) copy-start(bf16[128,1024]{1,0:T(8,128)(2,1)} %copy-done.24) | copy-start | bytes 786436
  832.1 14.1 %copy-start.47 = (f32[1024]{0:T(1024)S(1)}, f32[1024]{0:T(1024)}, u32[]{:S(2)}) copy-start(f32[1024]{0:T(1024)} %param.28) | copy-start | bytes 12292
  846.1 46.3 %copy-start.22 = (bf16[16,4096]{1,0:T(8,128)(2,1)S(1)}, bf16[16,4096]{1,0:T(8,128)(2,1)}, u32[]{:S(2)}) copy-start(bf16[16,4096]{1,0:T(8,128)(2,1)} %param.19) | copy-start | bytes 393220
  846.1 47.4 %copy-start.40 = (f32[4096]{0:T(1024)S(1)}, f32[4096]{0:T(1024)}, u32[]{:S(2)}) copy-start(f32[4096]{0:T(1024)} %param.30) | copy-start | bytes 49156
  851.8 90.4 %all-gather.8.cloned.1.call-start = ((), (), s32[]{:S(2)}) async-start(), calls=%async_computation.9 | async-start | bytes 4718592 | tf_op jit(solution)/shard_map/all_gather | solution.py:118
  912.8 94.1 %reduce-scatter.5.cloned.1.call-start = ((), (), s32[]{:S(2)}) async-start(), calls=%async_computation.10 | async-start | bytes 4718592 | tf_op jit(solution)/shard_map/reduce_scatter | solution.py:124
  952.3 74.9 %copy-start.1 = (bf16[1024,288]{0,1:T(8,128)(2,1)S(1)}, bf16[1024,288]{0,1:T(8,128)(2,1)}, u32[]{:S(2)}) copy-start(bf16[1024,288]{0,1:T(8,128)(2,1)} %param.24) | copy-start | bytes 1769476
  969.0 47.0 %copy-start.44 = (f32[16,2]{0,1:T(2,128)S(1)}, f32[16,2]{0,1:T(2,128)}, u32[]{:S(2)}) copy-start(f32[16,2]{0,1:T(2,128)} %param.32) | copy-start | bytes 388
  969.0 57.2 %copy-start.23 = (bf16[16,4096]{1,0:T(8,128)(2,1)S(1)}, bf16[16,4096]{1,0:T(8,128)(2,1)}, u32[]{:S(2)}) copy-start(bf16[16,4096]{1,0:T(8,128)(2,1)} %reduce-scatter.3.cloned.1.call-done) | copy-start | bytes 393220
  1009.0 17.1 %all-to-all-start.2 = ((bf16[16,4,4096]{2,1,0:T(4,128)(2,1)}), bf16[16,4,4096]{2,1,0:T(4,128)(2,1)S(1)}, u32[]{:S(2)}, u32[]{:S(2)}) async-start(bf16[16,4,4096]{2,1,0:T(4,128)(2,1)} %reshape.91), calls=%async_computation.4 | async-start | bytes 1048576 | tf_op jit(solution)/shard_map/all_to_all | solution.py:130
  (24 other events, 106.3 us)
Sparse Core Ops, SparseCore 0:
  25.2 24.8 all-gather.3
  287.5 61.9 all-reduce.29
  852.0 40.3 reduce-scatter.2
  913.0 29.2 all-gather.7
  969.1 37.7 reduce-scatter.4
Sparse Core Ops, SparseCore 1:
  290.2 79.9 all-gather.5
